TPU v7x, 32 devices: a whole 2x2x4 slice. The times are simulated.
32 devices in a mesh: row: 8 (over z, y), col: 4 (over x, core).
Axes of the slice: x: 2, y: 2, z: 4, core: 2. Of those that a mesh axis runs over, the one named last changes fastest.
Arguments:
- a_weights: bfloat16 [4096, 1024], P('row', 'col'), may hold values from 0.0001 to 1, as said below
- tile_mask: int32 [8, 2], replicated, may hold values from 0 to 1, as said below
- pair_mask: int32 [8, 8], replicated, may hold values from 0 to 1, as said below
Outputs:
- jaccard: bfloat16 [4096, 4096], P('row', 'col')
Inputs may be any that keep to these rules, and one draw needn't show every extreme that they name: `a_weights`: all weights positive. `tile_mask`: 1 where a tile is present; tile (I, I mod 2) of every block row I is present. `pair_mask`: symmetric, with ones on the diagonal.
All inputs are finite; a program needn't handle non-finite values.
Results may differ from a plain program's by a relative error of at most 0.001.
Values may be sent and summed in bfloat16 or wider, within the bound.
A program may use at most 64 MiB of HBM per device.

v0:
```python
import jax
import jax.numpy as jnp
from jax import lax
from jax.sharding import PartitionSpec as P

BLOCK = 512


def broadcast(value, axis, source):
    kept = jnp.where(lax.axis_index(axis) == source, value, 0).astype(value.dtype)
    return lax.psum(kept, axis)


def expand_tiles(flags):
    return jnp.repeat(jnp.repeat(flags, BLOCK, axis=0), BLOCK, axis=1)


def body(a_weights, tile_mask, pair_mask):
    row_index = lax.axis_index("row")
    col_index = lax.axis_index("col")
    pair_count = lax.axis_size("row") // lax.axis_size("col")
    blocks_here = a_weights.shape[0] // BLOCK
    own_flags = lax.dynamic_slice_in_dim(tile_mask, row_index * blocks_here, blocks_here, 0)
    own_mask = expand_tiles(own_flags).astype(jnp.bfloat16)
    gathered = lax.all_gather(a_weights, "col", axis=1, tiled=True)
    own_panel = gathered * own_mask
    row_degree = jnp.einsum("ik,ik->i", own_panel, own_panel, preferred_element_type=jnp.float32)
    remotes = [
        broadcast(own_panel, "row", pair_count * col_index + offset) for offset in range(pair_count)
    ]
    outputs = []
    for offset in range(pair_count):
        col_first = (pair_count * col_index + offset) * blocks_here
        remote = remotes[offset]
        pair_tiles = lax.dynamic_slice(
            pair_mask, (row_index * blocks_here, col_first), (blocks_here, blocks_here)
        )
        pair_open = expand_tiles(pair_tiles) > 0
        col_degree = jnp.einsum("ik,ik->i", remote, remote, preferred_element_type=jnp.float32)
        shared = lax.dot_general(
            own_panel, remote, (((1,), (1,)), ((), ())), preferred_element_type=jnp.float32
        )
        weights = shared / (row_degree[:, None] + col_degree[None, :] - shared)
        outputs.append(jnp.where(pair_open, weights, jnp.zeros_like(weights)))
    return jnp.concatenate(outputs, axis=1).astype(jnp.bfloat16)


def solution(mesh):
    in_specs = (P("row", "col"), P(), P())
    out_specs = P("row", "col")
    return jax.shard_map(body, mesh=mesh, in_specs=in_specs, out_specs=out_specs, check_vma=False)
```

profile of v0, /device:TPU:0, one launch (start us, length us, event | category | flops | bytes accessed | tf_op | source)
XLA Modules:
  0.0 146.8 jit_solution(6093091236768662315)
XLA Ops:
  6.5 0.0 all-gather.2.cloned.1.call-start
  6.5 0.7 all-gather.2.cloned.1.call-update
  7.3 0.0 all-reduce.3.cloned.1.call-start
  7.3 0.9 fusion.17
  8.2 0.1 broadcast_bitcast_fusion
  8.3 20.2 %all-gather.2.cloned.1.call-done = bf16[512,1024]{1,0:T(8,128)(2,1)} async-done(((bf16[512,256]{1,0:T(8,128)(2,1)}), bf16[512,1024]{1,0:T(8,128)(2,1)}) %all-gather.2.cloned.1.call-update) | async-done | bytes 1048592 | tf_op jit(solution)/shard_map/all_gather | solution.py:25
  28.5 2.7 %broadcast_select_fusion.1 = (bf16[512,1024]{1,0:T(8,128)(2,1)}, bf16[512,1024]{1,0:T(8,128)(2,1)}) fusion(pred[]{:T(512)S(6)} %eq.6, bf16[512,1024]{1,0:T(8,128)(2,1)} %all-gather.2.cloned.1.call-done, bf16[1024]{0:T(1024)(128)(2,1)S(1)} %bitcast.7, pred[]{:T(512)S(6)} %eq.7), kind=kLoop, calls=%fused_computation.14 | loop fusion | flops 1572864 | bytes 3147778 | tf_op jit(solution)/shard_map/jit(_where)/select_n | solution.py:10
  31.2 0.0 copy-start
  31.2 0.0 all-reduce.3.cloned.1.call-update
  31.2 1.5 fusion.18
  34.0 0.0 copy-done
  34.0 0.3 fusion.2
  34.3 100.0 %all-reduce.3.cloned.1.call-done = (bf16[512,1024]{1,0:T(8,128)(2,1)}, bf16[512,1024]{1,0:T(8,128)(2,1)}) async-done(((bf16[512,1024]{1,0:T(8,128)(2,1)}, bf16[512,1024]{1,0:T(8,128)(2,1)}), (bf16[512,1024]{1,0:T(8,128)(2,1)}, bf16[512,1024]{1,0:T(8,128)(2,1)})) %all-reduce.3.cloned.1.call-update) | async-done | bytes 2097168 | tf_op jit(solution)/shard_map/psum | solution.py:11
  134.4 0.0 copy-start.2
  134.4 2.1 %fusion = (f32[512]{0:T(512)S(1)}, f32[512]{0:T(512)S(1)}) fusion(bf16[512,1024]{1,0:T(8,128)(2,1)} %get-tuple-element.5, bf16[512,1024]{1,0:T(8,128)(2,1)} %get-tuple-element.6), kind=kLoop, calls=%fused_computation.1 | loop fusion | flops 3144704 | bytes 2101248 | tf_op jit(solution)/shard_map/ik,ik->i/dot_general | solution.py:39
  136.5 0.0 copy-done.2
  136.5 0.0 copy-start.1
  136.5 0.8 fusion.4
  137.3 0.4 copy-done.1
  137.7 0.8 fusion.6
  138.5 0.1 pad_maximum_fusion
  138.6 1.3 copy.4
  (1 shorter events, 0.0 us)
Async XLA Ops:
  6.5 21.9 %all-gather.2.cloned.1.call-start = ((), (), s32[]{:S(2)}) async-start(), calls=%async_computation | async-start | bytes 1310720 | tf_op jit(solution)/shard_map/all_gather | solution.py:25
  7.3 127.1 %all-reduce.3.cloned.1.call-start = ((), (), s32[]{:S(2)}) async-start(), calls=%async_computation.1 | async-start | bytes 4194304 | tf_op jit(solution)/shard_map/psum | solution.py:11
  31.2 2.8 %copy-start = (bf16[512,1024]{1,0:T(8,128)(2,1)S(1)}, bf16[512,1024]{1,0:T(8,128)(2,1)}, u32[]{:S(2)}) copy-start(bf16[512,1024]{1,0:T(8,128)(2,1)} %all-gather.2.cloned.1.call-done) | copy-start | bytes 3145732
  134.4 2.1 %copy-start.2 = (bf16[512,1024]{1,0:T(8,128)(2,1)S(1)}, bf16[512,1024]{1,0:T(8,128)(2,1)}, u32[]{:S(2)}) copy-start(bf16[512,1024]{1,0:T(8,128)(2,1)} %get-tuple-element.6) | copy-start | bytes 3145732
  136.5 1.2 copy-start.1
Sparse Core Ops, SparseCore 0:
  8.9 19.5 all-gather.1
  32.1 102.1 all-reduce.2
where the time goes:
time: 147 us
  waiting for transfers between devices  121 us (82%)
  between operations  14.8 us (10%)
  other arithmetic  6.09 us (4%)
  local copies, waits for them, and re-layouts  3.28 us (2%)
  matrix products  1.58 us (1%)
    psum x1, waiting for transfers between devices, broadcast(): return lax.psum(kept, axis)  100 us
    all_gather x1, waiting for transfers between devices, body(): gathered = lax.all_gather(a_weights, 'col', axis=1, tiled=True)  20.2 us
  transfers between devices with their start and end apart: 2, of which 2 were waited for; matrix products, arithmetic and copies ran while one was open for 2% of the time, Pallas kernels for 0%

commit v1 on v0

--- a/solution.py
+++ b/solution.py
@@ -8,7 +8,8 @@
 
 def broadcast(value, axis, source):
     kept = jnp.where(lax.axis_index(axis) == source, value, 0).astype(value.dtype)
-    return lax.psum(kept, axis)
+    step_on_meshes = lambda mine, row_axis: jnp.sum(lax.all_gather(mine, row_axis), axis=0)
+    return step_on_meshes(kept, axis)
 
 
 def expand_tiles(flags):

time: 147 us -> 297 us (2.02)
  waiting for transfers between devices: 121 us -> 262 us
  other arithmetic: 6.09 us -> 16 us
    all_gather x0 -> x2, waiting for transfers between devices: none -> 241 us  [broadcast(): lax.all_gather(mine, row_axis)]
    psum x1 -> x0, waiting for transfers between devices: 100 us -> none  [broadcast(): return lax.psum(kept, axis)]
    reduce_sum x0 -> x2, other arithmetic: none -> 11.3 us  [broadcast(): jnp.sum(lax.all_gather(mine, row_axis), axis=0)]
  transfers between devices with their start and end apart: 2 -> 3, of which waited for: 2 -> 3; matrix products, arithmetic and copies ran while one was open for 2% -> 3% of each run, Pallas kernels for 0% -> 0%
where the time goes in v1:
time: 297 us
  waiting for transfers between devices  262 us (88%)
  other arithmetic  16 us (5%)
  between operations  14.3 us (5%)
    all_gather x2, waiting for transfers between devices, broadcast(): lax.all_gather(mine, row_axis)  241 us
    all_gather x1, waiting for transfers between devices, body(): gathered = lax.all_gather(a_weights, 'col', axis=1, tiled=True)  20.2 us
    reduce_sum x2, other arithmetic, broadcast(): jnp.sum(lax.all_gather(mine, row_axis), axis=0)  11.3 us
  transfers between devices with their start and end apart: 3, of which 3 were waited for; matrix products, arithmetic and copies ran while one was open for 3% of the time, Pallas kernels for 0%

profile of v1, /device:TPU:0, one launch (start us, length us, event | category | flops | bytes accessed | tf_op | source)
XLA Modules:
  0.0 297.2 jit_solution(7134248792690212686)
XLA Ops:
  6.5 0.0 all-gather.6.cloned.1.call-start
  6.5 0.7 all-gather.6.cloned.1.call-update
  7.3 0.0 all-gather.8.cloned.1.call-start
  7.3 0.9 fusion.17
  8.2 0.1 broadcast_bitcast_fusion
  8.3 20.2 %all-gather.6.cloned.1.call-done = bf16[512,1024]{1,0:T(8,128)(2,1)} async-done(((bf16[512,256]{1,0:T(8,128)(2,1)}), bf16[512,1024]{1,0:T(8,128)(2,1)}) %all-gather.6.cloned.1.call-update) | async-done | bytes 1048592 | tf_op jit(solution)/shard_map/all_gather | solution.py:26
  28.5 0.0 copy-start
  28.5 2.8 broadcast_select_fusion.1
  31.3 0.0 all-gather.8.cloned.1.call-update
  31.3 0.0 all-gather.10.cloned.1.call-start
  31.3 0.7 all-gather.10.cloned.1.call-update
  32.0 1.4 fusion.18
  34.6 0.0 copy-done
  34.6 0.3 fusion.2
  34.9 121.5 %all-gather.8.cloned.1.call-done = bf16[4096,1024]{1,0:T(8,128)(2,1)} async-done(((bf16[512,1024]{1,0:T(8,128)(2,1)}), bf16[4096,1024]{1,0:T(8,128)(2,1)}) %all-gather.8.cloned.1.call-update) | async-done | bytes 8388624 | tf_op jit(solution)/shard_map/all_gather | solution.py:11
  156.4 5.7 %reduce_sum.24 = bf16[512,1024]{1,0:T(8,128)(2,1)S(1)} reduce(bf16[8,512,1024]{2,1,0:T(8,128)(2,1)} %bitcast.9, bf16[]{:T(256)} %constant.26.clone.1), dimensions={0}, to_apply=%region_0.1 | reduce | flops 3670016 | bytes 9437186 | tf_op jit(solution)/shard_map/reduce_sum | solution.py:11
  162.1 0.3 fusion.1
  162.3 119.3 %all-gather.10.cloned.1.call-done = bf16[4096,1024]{1,0:T(8,128)(2,1)} async-done(((bf16[512,1024]{1,0:T(8,128)(2,1)}), bf16[4096,1024]{1,0:T(8,128)(2,1)}) %all-gather.10.cloned.1.call-update) | async-done | bytes 8388624 | tf_op jit(solution)/shard_map/all_gather | solution.py:11
  281.7 5.7 %reduce_sum.25 = bf16[512,1024]{1,0:T(8,128)(2,1)S(1)} reduce(bf16[8,512,1024]{2,1,0:T(8,128)(2,1)} %bitcast.10, bf16[]{:T(256)} %constant.26.clone.1), dimensions={0}, to_apply=%region_1.2 | reduce | flops 3670016 | bytes 9437186 | tf_op jit(solution)/shard_map/reduce_sum | solution.py:11
  287.4 0.3 fusion
  287.6 0.8 fusion.4
  288.4 0.8 fusion.6
  289.2 0.1 pad_maximum_fusion
  289.3 1.3 copy.4
  (1 shorter events, 0.0 us)
Async XLA Ops:
  6.5 21.9 %all-gather.6.cloned.1.call-start = ((), (), s32[]{:S(2)}) async-start(), calls=%async_computation | async-start | bytes 1310720 | tf_op jit(solution)/shard_map/all_gather | solution.py:26
  7.3 149.1 %all-gather.8.cloned.1.call-start = ((), (), s32[]{:S(2)}) async-start(), calls=%async_computation.1 | async-start | bytes 9437184 | tf_op jit(solution)/shard_map/all_gather | solution.py:11
  28.5 6.1 %copy-start = (bf16[512,1024]{1,0:T(8,128)(2,1)S(1)}, bf16[512,1024]{1,0:T(8,128)(2,1)}, u32[]{:S(2)}) copy-start(bf16[512,1024]{1,0:T(8,128)(2,1)} %all-gather.6.cloned.1.call-done) | copy-start | bytes 3145732
  31.3 250.4 %all-gather.10.cloned.1.call-start = ((), (), s32[]{:S(2)}) async-start(), calls=%async_computation.2 | async-start | bytes 9437184 | tf_op jit(solution)/shard_map/all_gather | solution.py:11
Sparse Core Ops, SparseCore 0:
  8.9 19.5 all-gather.5
  31.4 124.9 all-gather.7
  158.5 123.1 all-gather.9

commit v2 on v0

--- a/solution.py
+++ b/solution.py
@@ -4,6 +4,12 @@
 from jax.sharding import PartitionSpec as P
 
 BLOCK = 512
+
+
+def track_screen(array_in, array_axis):
+    d_next = list(array_in.shape[1:])
+    d_next[array_axis] *= array_in.shape[0]
+    return jnp.moveaxis(array_in, 0, array_axis).reshape(d_next)
 
 
 def broadcast(value, axis, source):
@@ -22,7 +28,19 @@
     blocks_here = a_weights.shape[0] // BLOCK
     own_flags = lax.dynamic_slice_in_dim(tile_mask, row_index * blocks_here, blocks_here, 0)
     own_mask = expand_tiles(own_flags).astype(jnp.bfloat16)
-    gathered = lax.all_gather(a_weights, "col", axis=1, tiled=True)
+    devs = lax.axis_size("col")
+    steps_seen = tuple(((src_i, (src_i + 1) % devs) for src_i in range(devs)))
+    ready, passed = ([], [])
+    nodes = tuple(((k, k0) for k0, k in steps_seen))
+    for i in range(devs - 1):
+        if i % 2 == 0:
+            ready.append(lax.ppermute(ready[-1] if ready else a_weights, "col", steps_seen))
+        else:
+            passed.append(lax.ppermute(passed[-1] if passed else a_weights, "col", nodes))
+    plain = jnp.stack([*ready[::-1], a_weights, *passed])
+    mat_out = lax.axis_index("col") - len(ready)
+    plain = plain[(jnp.arange(devs) - mat_out) % devs]
+    gathered = track_screen(plain, 1)
     own_panel = gathered * own_mask
     row_degree = jnp.einsum("ik,ik->i", own_panel, own_panel, preferred_element_type=jnp.float32)
     remotes = [

time: 147 us -> 142 us (0.966)
  waiting for transfers between devices: 121 us -> 110 us
  starting transfers between devices: 0.04 us -> 5.07 us
  other arithmetic: 6.09 us -> 4.35 us
  matrix products: 1.58 us -> 3.09 us
    all_gather x1 -> x0, waiting for transfers between devices: 20.2 us -> none  [body(): gathered = lax.all_gather(a_weights, 'col', axis=1, tiled=True)]
    ppermute x0 -> x3, waiting for transfers between devices: none -> 6.54 us  [the longest x2 6.53 us: body(): lax.ppermute(ready[-1] if ready else a_weights, 'col', steps_seen)]
    ppermute x0 -> x3, starting transfers between devices: none -> 5.07 us  [the longest x2 3.14 us: body(): lax.ppermute(ready[-1] if ready else a_weights, 'col', steps_seen)]
    psum x1, waiting for transfers between devices: 100 us -> 104 us  [broadcast(): return lax.psum(kept, axis)]
    dot_general x1, other arithmetic: 2.11 us -> 0.44 us  [body(): jnp.einsum('ik,ik->i', remote, remote, preferred_element_type=jnp.float32)]
    dot_general x2, matrix products: 1.58 us -> 3.09 us  [body(): lax.dot_general(own_panel, remote, (((1,), (1,)), ((), ())), preferred_el...]
  transfers between devices with their start and end apart: 2 -> 4, of which waited for: 2 -> 3; matrix products, arithmetic and copies ran while one was open for 2% -> 2% of each run, Pallas kernels for 0% -> 0%
where the time goes in v2:
time: 142 us; the launch traced here: 141 us
  waiting for transfers between devices  110 us (77%)
  between operations  14.7 us (10%)
  starting transfers between devices  5.07 us (4%)
  other arithmetic  4.35 us (3%)
  local copies, waits for them, and re-layouts  4 us (3%)
  matrix products  3.09 us (2%)
    psum x1, waiting for transfers between devices, broadcast(): return lax.psum(kept, axis)  104 us
    ppermute x2, waiting for transfers between devices, body(): lax.ppermute(ready[-1] if ready else a_weights, 'col', steps_seen)  6.53 us
    ppermute x2, starting transfers between devices, body(): lax.ppermute(ready[-1] if ready else a_weights, 'col', steps_seen)  3.14 us
    dot_general x2, matrix products, body(): lax.dot_general(own_panel, remote, (((1,), (1,)), ((), ())), preferred_el...  3.09 us
  transfers between devices with their start and end apart: 4, of which 3 were waited for; matrix products, arithmetic and copies ran while one was open for 2% of the time, Pallas kernels for 0%

profile of v2, /device:TPU:0, one launch (start us, length us, event | category | flops | bytes accessed | tf_op | source)
XLA Modules:
  0.0 141.4 jit_solution(16317404627656041968)
XLA Ops:
  6.5 0.0 all-reduce.3.cloned.1.call-start
  6.5 0.5 collective-permute-start
  7.0 1.9 %collective-permute-start.2 = (bf16[512,256]{1,0:T(8,128)(2,1)}, bf16[512,256]{1,0:T(8,128)(2,1)S(1)}, u32[]{:S(2)}, u32[]{:S(2)}) collective-permute-start(bf16[512,256]{1,0:T(8,128)(2,1)} %param.3), channel_id=1, source_target_pairs={{1,0},{2,1},{3,2},{0,3},{5,4},{6,5},{7,6},{4,7},{9,8},{10,9},{11,1... | collective-permute-start | bytes 786440 | tf_op jit(solution)/shard_map/ppermute | solution.py:39
  8.9 0.9 fusion.7
  9.8 3.5 %collective-permute-done = bf16[512,256]{1,0:T(8,128)(2,1)S(1)} collective-permute-done((bf16[512,256]{1,0:T(8,128)(2,1)}, bf16[512,256]{1,0:T(8,128)(2,1)S(1)}, u32[]{:S(2)}, u32[]{:S(2)}) %collective-permute-start) | collective-permute-done | bytes 262176 | tf_op jit(solution)/shard_map/ppermute | solution.py:37
  13.3 2.7 %collective-permute-start.1 = (bf16[512,256]{1,0:T(8,128)(2,1)S(1)}, bf16[512,256]{1,0:T(8,128)(2,1)S(1)}, u32[]{:S(2)}, u32[]{:S(2)}) collective-permute-start(bf16[512,256]{1,0:T(8,128)(2,1)S(1)} %collective-permute-done), channel_id=1, source_target_pairs={{0,1},{1,2},{2,3},{3,0},{4,5},{5,6},{6,7},{7,4},{8,9},{9,10},{10,1... | collective-permute-start | bytes 786440 | tf_op jit(solution)/shard_map/ppermute | solution.py:37
  16.0 0.1 broadcast_bitcast_fusion
  16.1 0.0 collective-permute-done.2
  16.1 3.0 %collective-permute-done.1 = bf16[512,256]{1,0:T(8,128)(2,1)S(1)} collective-permute-done((bf16[512,256]{1,0:T(8,128)(2,1)S(1)}, bf16[512,256]{1,0:T(8,128)(2,1)S(1)}, u32[]{:S(2)}, u32[]{:S(2)}) %collective-permute-start.1) | collective-permute-done | bytes 262176 | tf_op jit(solution)/shard_map/ppermute | solution.py:37
  19.1 1.1 pad_maximum_fusion
  20.2 0.6 gather_fusion
  20.8 0.5 copy.6
  21.4 0.4 fusion.2
  21.8 1.5 %broadcast_select_fusion.1 = (bf16[512,1024]{0,1:T(8,128)(2,1)}, bf16[512,1024]{0,1:T(8,128)(2,1)}) fusion(bf16[512,1024]{0,1:T(8,128)(2,1)S(1)} %get-tuple-element.8, pred[]{:T(512)S(6)} %eq.8, pred[]{:T(512)S(6)} %eq.9), kind=kLoop, calls=%fused_computation.17 | loop fusion | flops 1048576 | bytes 3145730 | tf_op jit(solution)/shard_map/jit(_where)/select_n | solution.py:16
  23.3 0.0 all-reduce.3.cloned.1.call-update
  23.3 1.4 %fusion.10 = (s32[1,1]{1,0:T(1,128)}, s32[1,1]{1,0:T(1,128)}) fusion(s32[8,8]{1,0:T(8,128)} %param.5, s32[]{:T(128)S(6)} %select_n.56, s32[]{:T(128)S(6)} %select_n.57, s32[]{:T(128)S(6)} %select_n.63), kind=kLoop, calls=%fused_computation.28 | loop fusion | bytes 28 | tf_op jit(solution)/shard_map/dynamic_slice | solution.py:53
  26.0 103.5 %all-reduce.3.cloned.1.call-done = (bf16[512,1024]{0,1:T(8,128)(2,1)}, bf16[512,1024]{0,1:T(8,128)(2,1)}) async-done(((bf16[512,1024]{0,1:T(8,128)(2,1)}, bf16[512,1024]{0,1:T(8,128)(2,1)}), (bf16[512,1024]{0,1:T(8,128)(2,1)}, bf16[512,1024]{0,1:T(8,128)(2,1)})) %all-reduce.3.cloned.1.call-update) | async-done | bytes 2097168 | tf_op jit(solution)/shard_map/psum | solution.py:17
  129.5 0.0 copy-start
  129.5 0.0 copy-start.1
  129.5 2.1 %fusion.11 = f32[512,512]{0,1:T(8,128)S(1)} fusion(bf16[512,1024]{0,1:T(8,128)(2,1)S(1)} %get-tuple-element.8, bf16[512,1024]{0,1:T(8,128)(2,1)} %get-tuple-element.5), kind=kOutput, calls=%fused_computation.29 | convolution fusion | flops 536870912 | bytes 3145728 | tf_op jit(solution)/shard_map/dot_general | solution.py:58
  131.7 0.0 copy-done
  131.7 0.0 copy-done.1
  131.7 0.4 fusion
  132.1 1.0 fusion.4
  133.1 0.1 pad_maximum_fusion.1
  133.2 1.3 copy.7
  (3 shorter events, 0.0 us)
Async XLA Ops:
  6.5 123.0 %all-reduce.3.cloned.1.call-start = ((), (), s32[]{:S(2)}) async-start(), calls=%async_computation | async-start | bytes 4194304 | tf_op jit(solution)/shard_map/psum | solution.py:17
  6.5 6.8 %collective-permute-start = (bf16[512,256]{1,0:T(8,128)(2,1)}, bf16[512,256]{1,0:T(8,128)(2,1)S(1)}, u32[]{:S(2)}, u32[]{:S(2)}) collective-permute-start(bf16[512,256]{1,0:T(8,128)(2,1)} %param.3), channel_id=1, source_target_pairs={{0,1},{1,2},{2,3},{3,0},{4,5},{5,6},{6,7},{7,4},{8,9},{9,10},{10,1... | collective-permute-start | bytes 786440 | tf_op jit(solution)/shard_map/ppermute | solution.py:37
  7.0 9.1 %collective-permute-start.2 = (bf16[512,256]{1,0:T(8,128)(2,1)}, bf16[512,256]{1,0:T(8,128)(2,1)S(1)}, u32[]{:S(2)}, u32[]{:S(2)}) collective-permute-start(bf16[512,256]{1,0:T(8,128)(2,1)} %param.3), channel_id=1, source_target_pairs={{1,0},{2,1},{3,2},{0,3},{5,4},{6,5},{7,6},{4,7},{9,8},{10,9},{11,1... | collective-permute-start | bytes 786440 | tf_op jit(solution)/shard_map/ppermute | solution.py:39
  13.3 5.8 %collective-permute-start.1 = (bf16[512,256]{1,0:T(8,128)(2,1)S(1)}, bf16[512,256]{1,0:T(8,128)(2,1)S(1)}, u32[]{:S(2)}, u32[]{:S(2)}) collective-permute-start(bf16[512,256]{1,0:T(8,128)(2,1)S(1)} %collective-permute-done), channel_id=1, source_target_pairs={{0,1},{1,2},{2,3},{3,0},{4,5},{5,6},{6,7},{7,4},{8,9},{9,10},{10,1... | collective-permute-start | bytes 786440 | tf_op jit(solution)/shard_map/ppermute | solution.py:37
  129.5 2.1 %copy-start = (bf16[512,1024]{0,1:T(8,128)(2,1)S(1)}, bf16[512,1024]{0,1:T(8,128)(2,1)}, u32[]{:S(2)}) copy-start(bf16[512,1024]{0,1:T(8,128)(2,1)} %get-tuple-element.6) | copy-start | bytes 3145732
  129.5 2.1 %copy-start.1 = (bf16[512,1024]{0,1:T(8,128)(2,1)S(1)}, bf16[512,1024]{0,1:T(8,128)(2,1)}, u32[]{:S(2)}) copy-start(bf16[512,1024]{0,1:T(8,128)(2,1)} %get-tuple-element.5) | copy-start | bytes 3145732
Sparse Core Ops, SparseCore 0:
  23.4 106.0 all-reduce.2
